TPU v7x, 32 devices: a whole 2x2x4 slice. The times are simulated.
32 devices in a mesh: dp: 8 (over z, y), tensor: 4 (over x, core).
Axes of the slice: x: 2, y: 2, z: 4, core: 2. Of those that a mesh axis runs over, the one named last changes fastest.
Arguments:
- tokens: bfloat16 [16384, 768], P('dp'), may hold values from -6 to 6
- cotangent: bfloat16 [16384, 768], P('dp'), may hold values from -6 to 6
- row_lengths: int32 [32], P('dp'), may hold values from 64 to 512
- present: int32 [32, 64], P('dp'), may hold values 0 or 1
- groups: int32 [32, 512], P('dp'), may hold values from 0 to 63, never falling along the last dimension, each value on 1 to 16 neighbouring positions
- attn_weight: float32 [3, 768, 768], P(None, 'dp', 'tensor'), may hold values from -0.21875 to 0.21875
- attn_first: float32 [3, 768, 768], P(None, 'dp', 'tensor'), may hold values from -24 to 24
- attn_second: float32 [3, 768, 768], P(None, 'dp', 'tensor'), may hold values from 64 to 256
- mix_weight: float32 [768, 768], P('tensor', 'dp'), may hold values from -2.5 to 2.5
- mix_first: float32 [768, 768], P('tensor', 'dp'), may hold values from -32 to 32
- mix_second: float32 [768, 768], P('tensor', 'dp'), may hold values from 128 to 512
- up_weight: float32 [768, 3072], P('dp', 'tensor'), may hold values from -0.21875 to 0.21875
- up_first: float32 [768, 3072], P('dp', 'tensor'), may hold values from -96 to 96
- up_second: float32 [768, 3072], P('dp', 'tensor'), may hold values from 1024 to 4096
- down_weight: float32 [3072, 768], P('tensor', 'dp'), may hold values from -0.109375 to 0.109375
- down_first: float32 [3072, 768], P('tensor', 'dp'), may hold values from -192 to 192
- down_second: float32 [3072, 768], P('tensor', 'dp'), may hold values from 4096 to 16384
- head_bias: float32 [2, 768], P(None, ('tensor', 'dp')), may hold values from -4 to 4
- head_first: float32 [2, 768], P(None, ('tensor', 'dp')), may hold values from -512 to 512
- head_second: float32 [2, 768], P(None, ('tensor', 'dp')), may hold values from 8192 to 32768
- wide_bias: float32 [3072], P(('tensor', 'dp')), may hold values from -4 to 4
- wide_first: float32 [3072], P(('tensor', 'dp')), may hold values from -512 to 512
- wide_second: float32 [3072], P(('tensor', 'dp')), may hold values from 8192 to 32768
- norm_gains: float32 [2, 768], P(None, 'dp'), may hold values from 0.5 to 1.5
- gain_first: float32 [2, 768], P(None, 'dp'), may hold values from -512 to 512
- gain_second: float32 [2, 768], P(None, 'dp'), may hold values from 8192 to 32768
- shift_bias: float32 [4, 768], P(None, 'dp'), may hold values from -4 to 4
- shift_first: float32 [4, 768], P(None, 'dp'), may hold values from -512 to 512
- shift_second: float32 [4, 768], P(None, 'dp'), may hold values from 8192 to 32768
Outputs:
- layer_out: bfloat16 [16384, 768], P('dp')
- tokens_grad: bfloat16 [16384, 768], P('dp')
- attn_weight_new: float32 [3, 768, 768], P(None, 'dp', 'tensor')
- attn_first_new: float32 [3, 768, 768], P(None, 'dp', 'tensor')
- attn_second_new: float32 [3, 768, 768], P(None, 'dp', 'tensor')
- mix_weight_new: float32 [768, 768], P('tensor', 'dp')
- mix_first_new: float32 [768, 768], P('tensor', 'dp')
- mix_second_new: float32 [768, 768], P('tensor', 'dp')
- up_weight_new: float32 [768, 3072], P('dp', 'tensor')
- up_first_new: float32 [768, 3072], P('dp', 'tensor')
- up_second_new: float32 [768, 3072], P('dp', 'tensor')
- down_weight_new: float32 [3072, 768], P('tensor', 'dp')
- down_first_new: float32 [3072, 768], P('tensor', 'dp')
- down_second_new: float32 [3072, 768], P('tensor', 'dp')
- head_bias_new: float32 [2, 768], P(None, ('tensor', 'dp'))
- head_first_new: float32 [2, 768], P(None, ('tensor', 'dp'))
- head_second_new: float32 [2, 768], P(None, ('tensor', 'dp'))
- wide_bias_new: float32 [3072], P(('tensor', 'dp'))
- wide_first_new: float32 [3072], P(('tensor', 'dp'))
- wide_second_new: float32 [3072], P(('tensor', 'dp'))
- norm_gains_new: float32 [2, 768], P(None, 'dp')
- gain_first_new: float32 [2, 768], P(None, 'dp')
- gain_second_new: float32 [2, 768], P(None, 'dp')
- shift_bias_new: float32 [4, 768], P(None, 'dp')
- shift_first_new: float32 [4, 768], P(None, 'dp')
- shift_second_new: float32 [4, 768], P(None, 'dp')
- norm_pairs: float32 [2, 15], replicated
Inputs may be any that keep to these rules, and one draw needn't show every extreme that they name: Along a row the group ids never fall; every one of the 64 groups holds 1 to 16 slots.
All inputs are finite; a program needn't handle non-finite values. No bound on the sum of `present` on one device may be relied on, other than what follows from the above.
Results may differ from a plain program's by a relative error of at most 0.023.
Values may be sent and summed in bfloat16 or wider, within the bound.
No kernel may reach another device: no remote copies, remote signals or barrier semaphores. Data moves between devices by JAX's collectives and lax.ppermute only.
A program may use at most 128 MiB of HBM per device.

v0:
```python
from functools import partial
import jax
import jax.numpy as jnp
from jax import lax
from jax.sharding import PartitionSpec as P

HEAD = 64


def layer_norm(summed):
    center = summed - jnp.mean(summed, axis=-1, keepdims=True)
    spread = jnp.mean(center * center, axis=-1, keepdims=True)
    scaled = lax.rsqrt(spread + 1e-05)
    return (center * scaled, scaled)


def norm_back(upstream, normal, scaled):
    inner_sum = (
        upstream
        - jnp.mean(upstream, axis=-1, keepdims=True)
        - normal * jnp.mean(upstream * normal, axis=-1, keepdims=True)
    )
    return scaled * inner_sum


def visibility(length, present_row, group_row):
    positions = jnp.arange(group_row.shape[0])
    feature_ids = jnp.arange(present_row.shape[0])
    present_key = jnp.sum(
        (group_row[:, None] == feature_ids[None, :]) * present_row[None, :], axis=1
    )
    key_open = (positions < length) & (present_key == 1)
    return key_open[None, :] | (group_row[:, None] == group_row[None, :])


def row_scores(queries, key_rows, visible):
    scale = queries.shape[-1] ** (-0.5)
    scores = (
        jnp.einsum("qhd,khd->hqk", queries, key_rows, preferred_element_type=jnp.float32) * scale
    )
    return jnp.where(visible[None], scores, -1e30)


def row_forward(row_item):
    queries, key_rows, value_rows, visible = row_item
    scores = row_scores(queries, key_rows, visible)
    largest = jnp.max(scores, axis=-1, keepdims=True)
    exponent = jnp.exp(scores - largest)
    row_total = jnp.sum(exponent, axis=-1, keepdims=True)
    probs_low = (exponent / row_total).astype(jnp.bfloat16)
    context = jnp.einsum("hqk,khd->qhd", probs_low, value_rows, preferred_element_type=jnp.float32)
    return (context.astype(jnp.bfloat16), largest + jnp.log(row_total))


def row_backward(row_item):
    queries, key_rows, value_rows, visible, log_total, context_grad = row_item
    scale = queries.shape[-1] ** (-0.5)
    scores = row_scores(queries, key_rows, visible)
    softmax_probs = jnp.exp(scores - log_total)
    probs_low = softmax_probs.astype(jnp.bfloat16)
    value_grad = jnp.einsum(
        "hqk,qhd->khd", probs_low, context_grad, preferred_element_type=jnp.float32
    )
    probs_grad = jnp.einsum(
        "qhd,khd->hqk", context_grad, value_rows, preferred_element_type=jnp.float32
    )
    inner_sum = jnp.sum(softmax_probs * probs_grad, axis=-1, keepdims=True)
    scores_grad = (softmax_probs * (probs_grad - inner_sum)).astype(jnp.bfloat16)
    query_grad = (
        jnp.einsum("hqk,khd->qhd", scores_grad, key_rows, preferred_element_type=jnp.float32)
        * scale
    )
    key_grad = (
        jnp.einsum("hqk,qhd->khd", scores_grad, queries, preferred_element_type=jnp.float32) * scale
    )
    return (
        query_grad.astype(jnp.bfloat16),
        key_grad.astype(jnp.bfloat16),
        value_grad.astype(jnp.bfloat16),
    )


def square_sums(array, piece_count, weight_factor):
    if piece_count == 1:
        return [jnp.sum(array * array) * weight_factor]
    return [jnp.sum(array[member] * array[member]) * weight_factor for member in range(piece_count)]


def trust_factor(trust, offset, piece_count, rank_count):
    if piece_count == 1:
        return trust[offset]
    return trust[offset : offset + piece_count].reshape((piece_count,) + (1,) * (rank_count - 1))


def on_device(
    tokens,
    cotangent,
    row_lengths,
    present,
    groups,
    attn_weight,
    attn_first,
    attn_second,
    mix_weight,
    mix_first,
    mix_second,
    up_weight,
    up_first,
    up_second,
    down_weight,
    down_first,
    down_second,
    head_bias,
    head_first,
    head_second,
    wide_bias,
    wide_first,
    wide_second,
    norm_gains,
    gain_first,
    gain_second,
    shift_bias,
    shift_first,
    shift_second,
):
    bfloat = jnp.bfloat16
    single = jnp.float32
    attn_low, mix_low, up_low, down_low, head_low, wide_low, gain_low, shift_low = (
        lax.all_gather(attn_weight.astype(bfloat), "dp", axis=1, tiled=True),
        lax.all_gather(mix_weight.astype(bfloat), "dp", axis=1, tiled=True),
        lax.all_gather(up_weight.astype(bfloat), "dp", axis=0, tiled=True),
        lax.all_gather(down_weight.astype(bfloat), "dp", axis=1, tiled=True),
        lax.all_gather(head_bias.astype(bfloat), "dp", axis=1, tiled=True),
        lax.all_gather(wide_bias.astype(bfloat), "dp", axis=0, tiled=True),
        lax.all_gather(norm_gains.astype(bfloat), "dp", axis=1, tiled=True),
        lax.all_gather(shift_bias.astype(bfloat), "dp", axis=1, tiled=True),
    )
    gain_float = gain_low.astype(single)
    shift_float = shift_low.astype(single)
    row_count = row_lengths.shape[0]
    row_slots = groups.shape[1]
    local_width = attn_low.shape[2]
    row_shape = (row_count, row_slots, local_width // HEAD, HEAD)
    projected = jnp.einsum("td,kdc->ktc", tokens, attn_low, preferred_element_type=single)
    queries = (projected[0] + head_low[0].astype(single)).astype(bfloat).reshape(row_shape)
    key_rows = projected[1].astype(bfloat).reshape(row_shape)
    value_rows = (projected[2] + head_low[1].astype(single)).astype(bfloat).reshape(row_shape)
    visible = jax.vmap(visibility)(row_lengths, present, groups)
    context, log_total = lax.map(row_forward, (queries, key_rows, value_rows, visible))
    context = context.reshape(row_count * row_slots, local_width)
    attn_part = jnp.dot(context, mix_low, preferred_element_type=single)
    attended = (
        lax.psum(attn_part.astype(jnp.bfloat16), "tensor").astype(jnp.float32) + shift_float[0]
    )
    normal_one, scaled_one = layer_norm(tokens.astype(single) + attended)
    normed = normal_one * gain_float[0] + shift_float[1]
    normed_low = normed.astype(bfloat)
    hidden = jnp.dot(normed_low, up_low, preferred_element_type=single) + wide_low.astype(single)
    active, gelu_back = jax.vjp(partial(jax.nn.gelu, approximate=False), hidden)
    active_low = active.astype(bfloat)
    ffn_part = jnp.dot(active_low, down_low, preferred_element_type=single)
    summed_two = (
        normed
        + lax.psum(ffn_part.astype(jnp.bfloat16), "tensor").astype(jnp.float32)
        + shift_float[2]
    )
    normal_two, scaled_two = layer_norm(summed_two)
    layer_out = (normal_two * gain_float[1] + shift_float[3]).astype(bfloat)
    upstream = cotangent.astype(single)
    gain_two_grad = jnp.sum(upstream * normal_two, axis=0)
    shift_three_grad = jnp.sum(upstream, axis=0)
    back_two = norm_back(upstream * gain_float[1], normal_two, scaled_two)
    shift_two_grad = jnp.sum(back_two, axis=0)
    back_two_low = back_two.astype(bfloat)
    down_grad = jnp.einsum("tf,td->fd", active_low, back_two_low, preferred_element_type=single)
    active_grad = jnp.einsum("td,fd->tf", back_two_low, down_low, preferred_element_type=single)
    hidden_grad = gelu_back(active_grad)[0].astype(bfloat)
    wide_grad = jnp.sum(hidden_grad.astype(single), axis=0)
    up_grad = jnp.einsum("td,tf->df", normed_low, hidden_grad, preferred_element_type=single)
    normed_part = jnp.einsum("tf,df->td", hidden_grad, up_low, preferred_element_type=single)
    normed_grad = back_two + lax.psum(normed_part.astype(jnp.bfloat16), "tensor").astype(
        jnp.float32
    )
    gain_one_grad = jnp.sum(normed_grad * normal_one, axis=0)
    shift_one_grad = jnp.sum(normed_grad, axis=0)
    back_one = norm_back(normed_grad * gain_float[0], normal_one, scaled_one)
    shift_zero_grad = jnp.sum(back_one, axis=0)
    back_one_low = back_one.astype(bfloat)
    mix_grad = jnp.einsum("tc,td->cd", context, back_one_low, preferred_element_type=single)
    context_grad = jnp.einsum(
        "td,cd->tc", back_one_low, mix_low, preferred_element_type=single
    ).astype(bfloat)
    query_grad, key_grad, value_grad = lax.map(
        row_backward,
        (queries, key_rows, value_rows, visible, log_total, context_grad.reshape(row_shape)),
    )
    token_count = row_count * row_slots
    stacked = jnp.stack(
        [
            query_grad.reshape(token_count, local_width),
            key_grad.reshape(token_count, local_width),
            value_grad.reshape(token_count, local_width),
        ]
    )
    head_grad = jnp.stack(
        [jnp.sum(stacked[0].astype(single), axis=0), jnp.sum(stacked[2].astype(single), axis=0)]
    )
    attn_grad = jnp.einsum("td,ktc->kdc", tokens, stacked, preferred_element_type=single)
    token_part = jnp.einsum("ktc,kdc->td", stacked, attn_low, preferred_element_type=single)
    tokens_grad = (
        back_one + lax.psum(token_part.astype(jnp.bfloat16), "tensor").astype(jnp.float32)
    ).astype(bfloat)
    gain_grad = jnp.stack([gain_one_grad, gain_two_grad])
    shift_grad = jnp.stack([shift_zero_grad, shift_one_grad, shift_two_grad, shift_three_grad])
    attn_sum_grad, mix_sum, up_sum, down_sum, head_sum, wide_sum, gain_sum, shift_sum = (
        lax.psum_scatter(attn_grad, "dp", scatter_dimension=1, tiled=True),
        lax.psum_scatter(mix_grad, "dp", scatter_dimension=1, tiled=True),
        lax.psum_scatter(up_grad, "dp", scatter_dimension=0, tiled=True),
        lax.psum_scatter(down_grad, "dp", scatter_dimension=1, tiled=True),
        lax.psum_scatter(head_grad, "dp", scatter_dimension=1, tiled=True),
        lax.psum_scatter(wide_grad, "dp", scatter_dimension=0, tiled=True),
        lax.psum_scatter(gain_grad, "dp", scatter_dimension=1, tiled=True),
        lax.psum_scatter(shift_grad, "dp", scatter_dimension=1, tiled=True),
    )
    masters = (
        attn_weight,
        mix_weight,
        up_weight,
        down_weight,
        head_bias,
        wide_bias,
        norm_gains,
        shift_bias,
    )
    firsts = (
        attn_first,
        mix_first,
        up_first,
        down_first,
        head_first,
        wide_first,
        gain_first,
        shift_first,
    )
    seconds = (
        attn_second,
        mix_second,
        up_second,
        down_second,
        head_second,
        wide_second,
        gain_second,
        shift_second,
    )
    reduced = (attn_sum_grad, mix_sum, up_sum, down_sum, head_sum, wide_sum, gain_sum, shift_sum)
    piece_counts = (3, 1, 1, 1, 2, 1, 2, 4)
    share = 1.0 / lax.axis_size("tensor")
    weight_factors = (1.0, 1.0, 1.0, 1.0, 1.0, 1.0, share, share)
    new_firsts, new_seconds, updates, weight_sq, update_sq = ([], [], [], [], [])
    for master, first_old, second_old, gradient, piece_count, weight_factor in zip(
        masters, firsts, seconds, reduced, piece_counts, weight_factors
    ):
        first_new = 0.5 * first_old + 0.5 * gradient
        second_new = 0.5 * second_old + 0.5 * gradient * gradient
        update = first_new / (jnp.sqrt(second_new) + 1e-06) + 0.01 * master
        new_firsts.append(first_new)
        new_seconds.append(second_new)
        updates.append(update)
        weight_sq.extend(square_sums(master, piece_count, weight_factor))
        update_sq.extend(square_sums(update, piece_count, weight_factor))
    square_totals = lax.psum(
        jnp.stack([jnp.stack(weight_sq), jnp.stack(update_sq)]), ("dp", "tensor")
    )
    norm_pairs = jnp.sqrt(square_totals)
    trust = norm_pairs[0] / (norm_pairs[1] + 1e-06)
    new_masters = []
    offset = 0
    for master, update, piece_count in zip(masters, updates, piece_counts):
        factor = trust_factor(trust, offset, piece_count, master.ndim)
        new_masters.append(master - 0.5 * factor * update)
        offset = offset + piece_count
    return (
        layer_out,
        tokens_grad,
        new_masters[0],
        new_firsts[0],
        new_seconds[0],
        new_masters[1],
        new_firsts[1],
        new_seconds[1],
        new_masters[2],
        new_firsts[2],
        new_seconds[2],
        new_masters[3],
        new_firsts[3],
        new_seconds[3],
        new_masters[4],
        new_firsts[4],
        new_seconds[4],
        new_masters[5],
        new_firsts[5],
        new_seconds[5],
        new_masters[6],
        new_firsts[6],
        new_seconds[6],
        new_masters[7],
        new_firsts[7],
        new_seconds[7],
        norm_pairs,
    )


def solution(mesh):
    return jax.shard_map(
        on_device,
        mesh=mesh,
        in_specs=(
            P("dp", None),
            P("dp", None),
            P("dp"),
            P("dp", None),
            P("dp", None),
            P(None, "dp", "tensor"),
            P(None, "dp", "tensor"),
            P(None, "dp", "tensor"),
            P("tensor", "dp"),
            P("tensor", "dp"),
            P("tensor", "dp"),
            P("dp", "tensor"),
            P("dp", "tensor"),
            P("dp", "tensor"),
            P("tensor", "dp"),
            P("tensor", "dp"),
            P("tensor", "dp"),
            P(None, ("tensor", "dp")),
            P(None, ("tensor", "dp")),
            P(None, ("tensor", "dp")),
            P(("tensor", "dp")),
            P(("tensor", "dp")),
            P(("tensor", "dp")),
            P(None, "dp"),
            P(None, "dp"),
            P(None, "dp"),
            P(None, "dp"),
            P(None, "dp"),
            P(None, "dp"),
        ),
        out_specs=(
            P("dp", None),
            P("dp", None),
            P(None, "dp", "tensor"),
            P(None, "dp", "tensor"),
            P(None, "dp", "tensor"),
            P("tensor", "dp"),
            P("tensor", "dp"),
            P("tensor", "dp"),
            P("dp", "tensor"),
            P("dp", "tensor"),
            P("dp", "tensor"),
            P("tensor", "dp"),
            P("tensor", "dp"),
            P("tensor", "dp"),
            P(None, ("tensor", "dp")),
            P(None, ("tensor", "dp")),
            P(None, ("tensor", "dp")),
            P(("tensor", "dp")),
            P(("tensor", "dp")),
            P(("tensor", "dp")),
            P(None, "dp"),
            P(None, "dp"),
            P(None, "dp"),
            P(None, "dp"),
            P(None, "dp"),
            P(None, "dp"),
            P(),
        ),
        check_vma=False,
    )
```

profile of v0, /device:TPU:0, one launch (start us, length us, event | category | flops | bytes accessed | tf_op | source)
XLA Modules:
  0.0 908.2 jit_solution(8584713637614694734)
XLA Ops:
  9.2 38.6 %all_gather.24 = bf16[3,768,192]{2,0,1:T(4,128)(2,1)S(1)} all-gather(bf16[3,96,192]{2,0,1:T(4,128)(2,1)S(1)} %copy.160), channel_id=1, replica_groups=mesh['dp'=8,'tensor'=4] {'dp'}, dimensions={1}, use_global_device_ids=true | all-gather | bytes 995328 | tf_op jit(solution)/shard_map/all_gather | solution.py:129
  47.8 5.2 convolution_bitcast_fusion
  54.4 2.2 squeeze.31
  56.6 2.2 squeeze.32
  58.8 18.9 %all-gather = bf16[8,24,2]{1,2,0:T(2,128)(2,1)S(1)} all-gather(bf16[1,24,2]{1,2,0:T(2,128)(2,1)S(1)} %convert_bitcast_fusion.2), channel_id=1, replica_groups=mesh['dp'=8,'tensor'=4] {'dp'}, dimensions={0}, use_global_device_ids=true | all-gather | bytes 864 | tf_op jit(solution)/shard_map/all_gather | solution.py:133
  78.0 2.3 convert_element_type.154
  81.6 2.9 fusion.72
  85.5 15.5 %while.26 = (s32[]{:T(128)}, bf16[4,512,3,64]{1,3,2,0:T(8,128)(2,1)}, f32[4,3,512,1]{2,1,3,0:T(4,128)}, bf16[4,512,3,64]{1,3,2,0:T(8,128)(2,1)S(1)}, pred[4,512,...) while((s32[]{:T(128)}, ...), condition=%wide.region_4.5_spmd, body=%wide.region_1.4_spmd.sunk | while | flops 210860544 | bytes 11592281 | solution.py:149
  108.4 31.2 %all_gather.26 = bf16[192,768]{0,1:T(8,128)(2,1)S(1)} all-gather(bf16[192,96]{0,1:T(8,128)(2,1)} %copy.167), channel_id=1, replica_groups=mesh['dp'=8,'tensor'=4] {'dp'}, dimensions={1}, use_global_device_ids=true | all-gather | bytes 331776 | tf_op jit(solution)/shard_map/all_gather | solution.py:130
  139.6 3.9 convolution_convert_fusion.2
  147.0 16.5 %all-gather.1 = bf16[8,96,4]{1,2,0:T(4,128)(2,1)S(1)} all-gather(bf16[1,96,4]{1,2,0:T(4,128)(2,1)S(1)} %convert_bitcast_fusion), channel_id=1, replica_groups=mesh['dp'=8,'tensor'=4] {'dp'}, dimensions={0}, use_global_device_ids=true | all-gather | bytes 6912 | tf_op jit(solution)/shard_map/all_gather | solution.py:136
  166.4 18.0 %all-gather.2 = bf16[8,96,2]{1,2,0:T(2,128)(2,1)S(1)} all-gather(bf16[1,96,2]{1,2,0:T(2,128)(2,1)S(1)} %convert_bitcast_fusion.1), channel_id=1, replica_groups=mesh['dp'=8,'tensor'=4] {'dp'}, dimensions={0}, use_global_device_ids=true | all-gather | bytes 3456 | tf_op jit(solution)/shard_map/all_gather | solution.py:135
  189.9 17.7 %all-reduce = bf16[768]{0:T(1024)(128)(2,1)S(1)} all-reduce(bf16[768]{0:T(1024)(128)(2,1)S(1)} %dynamic-update-slice), channel_id=1, replica_groups=mesh['dp'=8,'tensor'=4] {'dp'}, use_global_device_ids=true, to_apply=%add | all-reduce | flops 768 | bytes 3072
  209.3 3.1 fusion.68
  214.9 20.6 %multiply_convert_fusion.1 = (bf16[2048,768]{1,0:T(8,128)(2,1)}, f32[2048,768]{1,0:T(8,128)}, f32[2048,768]{1,0:T(8,128)}) fusion(f32[768]{0:T(1024)} %convert_element_type.165, bf16[768,768]{1,0:T(8,128)(2,1)} %all-gather.6.cloned.1.call-done, f32[768]{0:T(1024)} %get-tuple-element.367, f32[768]{0:T(1024)S(1)} %get-tuple-element.370, ...), kind=kOutput, calls=%fused_computation.83 | convolution fusion | flops 2533883904 | bytes 23228416 | tf_op jit(solution)/shard_map/dot_general | solution.py:158
  235.4 6.5 convolution_convert_fusion.1
  242.3 68.4 %all-reduce.11.cloned.1.call-done = bf16[2048,768]{1,0:T(8,128)(2,1)} async-done(((bf16[2048,768]{1,0:T(8,128)(2,1)}), bf16[2048,768]{1,0:T(8,128)(2,1)}) %all-reduce.11.cloned.1.call-update) | async-done | bytes 3145744 | tf_op jit(solution)/shard_map/psum | solution.py:164
  310.7 4.8 fusion.119
  317.4 3.6 fusion.61
  321.1 3.8 fusion.58
  324.9 9.4 %convert_reduce_fusion.1 = (f32[768]{0:T(1024)}, bf16[2048,768]{1,0:T(8,128)(2,1)S(1)}) fusion(f32[2048,768]{1,0:T(8,128)S(1)} %bitcast.250, bf16[768,768]{0,1:T(8,128)(2,1)S(1)} %copy-done.57, f32[2048,768]{1,0:T(8,128)S(1)} %get-tuple-element.457, f32[2048,768]{1,0:T(8,128)} %get-tuple-element.471, f32[768]{0:T(1024)S(1)} %copy-done.43), kind=kOutput, calls=%fused_computation.74 | convolution fusion | flops 2444229888 | bytes 23205888 | tf_op jit(solution)/shard_map/td,fd->tf/dot_general | solution.py:176
  335.9 4.0 convolution_convert_fusion
  342.6 66.1 %all-reduce.13.cloned.1.call-done = bf16[2048,768]{1,0:T(8,128)(2,1)} async-done(((bf16[2048,768]{1,0:T(8,128)(2,1)}), bf16[2048,768]{1,0:T(8,128)(2,1)}) %all-reduce.13.cloned.1.call-update) | async-done | bytes 3145744 | tf_op jit(solution)/shard_map/psum | solution.py:181
  408.7 7.3 multiply_reduce_fusion.1
  416.0 8.1 fusion.111
  431.7 5.3 fusion.86
  437.1 7.7 fusion.91
  444.8 7.9 fusion.77
  452.8 4.9 convolution_convert_fusion.3
  457.7 3.1 reshape.246
  460.8 2.2 copy.171
  465.9 51.0 %while.27 = (s32[]{:T(128)}, bf16[4,512,3,64]{1,3,2,0:T(8,128)(2,1)}, bf16[4,512,3,64]{1,3,2,0:T(8,128)(2,1)}, bf16[4,512,3,64]{1,3,2,0:T(8,128)(2,1)}, bf16[4,5...) while((s32[]{:T(128)}, ...), condition=%wide.region_18.19_spmd, body=%wide.region_16.18_spmd.sunk | while | flops 510884352 | bytes 26381428 | solution.py:193
  469.3 2.2 multiply_reduce_fusion.34
  472.3 2.2 fusion.170
  476.5 2.2 fusion.171
  482.0 2.2 multiply_reduce_fusion.34
  485.0 2.2 fusion.170
  489.2 2.2 fusion.171
  494.8 2.2 multiply_reduce_fusion.34
  497.8 2.2 fusion.170
  502.0 2.2 fusion.171
  507.5 2.2 multiply_reduce_fusion.34
  510.5 2.2 fusion.170
  514.7 2.2 fusion.171
  516.9 2.6 copy.172
  519.6 2.8 stack_reshape.9
  522.4 2.6 copy.173
  525.0 2.8 stack_reshape.10
  527.8 2.7 copy.174
  530.5 2.8 stack_reshape.11
  538.3 3.2 fusion.83
  541.5 3.2 copy.187
  544.7 2.8 reshape.264
  560.5 21.7 %all-reduce.3 = (f32[2,192]{1,0:T(2,128)S(1)}, f32[768]{0:T(1024)S(1)}) all-reduce(f32[2,192]{1,0:T(2,128)S(1)} %pad_maximum_fusion.2, f32[768]{0:T(1024)S(1)} %copy-done.42), channel_id=6, replica_groups=mesh['dp'=8,'tensor'=4] {'dp'}, use_global_device_ids=true, to_apply=%region_47.48.clone | all-reduce | flops 1152 | bytes 9216
  583.6 6.7 bitcast_convert_fusion
  599.7 19.1 %reduce-scatter.22.cloned.1.call-done = f32[96,192]{1,0:T(8,128)} async-done(((f32[768,192]{1,0:T(8,128)}), f32[96,192]{1,0:T(8,128)}) %reduce-scatter.22.cloned.1.call-update) | async-done | bytes 73744
  621.2 69.8 %reduce-scatter.16.cloned.1.call-done = f32[96,768]{1,0:T(8,128)} async-done(((f32[768,768]{1,0:T(8,128)}), f32[96,768]{1,0:T(8,128)}) %reduce-scatter.16.cloned.1.call-update) | async-done | bytes 294928 | tf_op jit(solution)/shard_map/reduce_scatter | solution.py:218
  692.8 70.3 %reduce-scatter.18.cloned.1.call-done = f32[768,96]{0,1:T(8,128)} async-done(((f32[768,768]{0,1:T(8,128)}), f32[768,96]{0,1:T(8,128)}) %reduce-scatter.18.cloned.1.call-update) | async-done | bytes 294928 | tf_op jit(solution)/shard_map/reduce_scatter | solution.py:219
  763.1 2.7 multiply_reduce_fusion.8
  765.8 6.3 stack.157
  772.0 60.6 %reduce-scatter.20.cloned.1.call-done = f32[96,576]{1,0:T(8,128)} async-done(((f32[768,576]{1,0:T(8,128)}), f32[96,576]{1,0:T(8,128)}) %reduce-scatter.20.cloned.1.call-update) | async-done | bytes 221200
  836.5 5.9 stack.185
  843.2 6.1 add_convert_fusion
  849.3 39.4 %psum.39 = f32[2,15]{1,0:T(2,128)S(1)} all-reduce(f32[2,15]{1,0:T(2,128)S(1)} %pad_maximum_fusion.3), channel_id=1, replica_groups=mesh['dp'=8,'tensor'=4] {'dp','tensor'}, use_global_device_ids=true, to_apply=%region_67.68 | all-reduce | flops 30 | bytes 240 | tf_op jit(solution)/shard_map/psum | solution.py:271
  (299 shorter events, 122.7 us)
Async XLA Ops:
  8.0 201.3 %all-reduce.9.cloned.1.call-start = ((), (), s32[]{:S(2)}) async-start(), calls=%async_computation.6 | async-start | bytes 6291456 | tf_op jit(solution)/shard_map/psum | solution.py:153
  47.8 5.6 copy-start.13
  53.0 5.8 copy-start.36
  53.4 27.1 %copy-start.29 = (s32[4,512]{1,0:T(4,128)S(1)}, s32[4,512]{1,0:T(4,128)}, u32[]{:S(2)}) copy-start(s32[4,512]{1,0:T(4,128)} %param.37) | copy-start | bytes 24580
  53.4 27.1 %copy-start.44 = (s32[4,64]{1,0:T(4,128)S(1)}, s32[4,64]{1,0:T(4,128)}, u32[]{:S(2)}) copy-start(s32[4,64]{1,0:T(4,128)} %param.36) | copy-start | bytes 3076
  53.4 27.2 %copy-start.55 = (s32[4]{0:T(128)S(1)}, s32[4]{0:T(128)}, u32[]{:S(2)}) copy-start(s32[4]{0:T(128)} %param.35) | copy-start | bytes 52
  85.5 22.2 %copy-start.18 = (f32[192,96]{1,0:T(8,128)S(1)}, f32[192,96]{1,0:T(8,128)}, u32[]{:S(2)}) copy-start(f32[192,96]{1,0:T(8,128)} %param.41) | copy-start | bytes 221188
  104.7 42.3 %copy-start.31 = (f32[4,96]{1,0:T(4,128)S(1)}, f32[4,96]{1,0:T(4,128)}, u32[]{:S(2)}) copy-start(f32[4,96]{1,0:T(4,128)} %param.59) | copy-start | bytes 4612
  104.7 104.7 %copy-start = (bf16[2048,768]{1,0:T(8,128)(2,1)S(1)}, bf16[2048,768]{1,0:T(8,128)(2,1)}, u32[]{:S(2)}) copy-start(bf16[2048,768]{1,0:T(8,128)(2,1)} %param.33) | copy-start | bytes 9437188
  143.4 71.4 %all-gather.6.cloned.1.call-start = ((), (), s32[]{:S(2)}) async-start(), calls=%async_computation.7 | async-start | bytes 1327104 | tf_op jit(solution)/shard_map/all_gather | solution.py:131
  145.2 90.3 %all-gather.8.cloned.1.call-start = ((), (), s32[]{:S(2)}) async-start(), calls=%async_computation.8 | async-start | bytes 1327104 | tf_op jit(solution)/shard_map/all_gather | solution.py:132
  146.9 163.8 %all-reduce.11.cloned.1.call-start = ((), (), s32[]{:S(2)}) async-start(), calls=%async_computation.9 | async-start | bytes 6291456 | tf_op jit(solution)/shard_map/psum | solution.py:164
  209.3 3.2 copy-start.1
  242.0 166.7 %all-reduce.13.cloned.1.call-start = ((), (), s32[]{:S(2)}) async-start(), calls=%async_computation.10 | async-start | bytes 6291456 | tf_op jit(solution)/shard_map/psum | solution.py:181
  316.4 4.6 copy-start.33
  317.4 7.5 slice-start
  321.0 3.8 copy-start.43
  321.0 3.8 copy-start.57
  321.1 3.8 slice-start.1
  324.9 9.4 %copy-start.3 = (f32[2048,768]{1,0:T(8,128)}, f32[2048,768]{1,0:T(8,128)S(1)}, u32[]{:S(2)}) copy-start(f32[2048,768]{1,0:T(8,128)S(1)} %get-tuple-element.457) | copy-start | bytes 18874372
  324.9 11.1 %copy-start.56 = (bf16[768,768]{1,0:T(8,128)(2,1)S(1)}, bf16[768,768]{1,0:T(8,128)(2,1)}, u32[]{:S(2)}) copy-start(bf16[768,768]{1,0:T(8,128)(2,1)} %all-gather.6.cloned.1.call-done) | copy-start | bytes 3538948
  340.0 251.7 %reduce-scatter.24.cloned.1.call-start = ((), (), s32[]{:S(2)}) async-start(), calls=%async_computation.16 | async-start | bytes 442368
  408.7 7.3 copy-start.2
  408.7 7.3 copy-start.8
  408.7 7.3 copy-start.26
  416.0 9.9 %copy-start.34 = (f32[1,768]{1,0:T(1,128)S(1)}, f32[1,768]{1,0:T(1,128)}, u32[]{:S(2)}) copy-start(f32[1,768]{1,0:T(1,128)} %stack.172) | copy-start | bytes 9220
  428.1 166.9 %reduce-scatter.26.cloned.1.call-start = ((), (), s32[]{:S(2)}) async-start(), calls=%async_computation.17 | async-start | bytes 442368
  431.2 187.7 %reduce-scatter.22.cloned.1.call-start = ((), (), s32[]{:S(2)}) async-start(), calls=%async_computation.15 | async-start | bytes 884736
  437.0 254.0 %reduce-scatter.16.cloned.1.call-start = ((), (), s32[]{:S(2)}) async-start(), calls=%async_computation.12 | async-start | bytes 2654208 | tf_op jit(solution)/shard_map/reduce_scatter | solution.py:218
  444.8 318.3 %reduce-scatter.18.cloned.1.call-start = ((), (), s32[]{:S(2)}) async-start(), calls=%async_computation.13 | async-start | bytes 2654208 | tf_op jit(solution)/shard_map/reduce_scatter | solution.py:219
  452.7 379.9 %reduce-scatter.20.cloned.1.call-start = ((), (), s32[]{:S(2)}) async-start(), calls=%async_computation.14 | async-start | bytes 2211840
  541.5 6.1 copy-start.10
  541.5 6.2 copy-start.32
  541.5 9.5 %copy-start.35 = (f32[2,96]{1,0:T(2,128)S(1)}, f32[2,96]{1,0:T(2,128)}, u32[]{:S(2)}) copy-start(f32[2,96]{1,0:T(2,128)} %param.56) | copy-start | bytes 2308
  541.5 14.9 %copy-start.37 = (f32[2,24]{1,0:T(2,128)S(1)}, f32[2,24]{1,0:T(2,128)}, u32[]{:S(2)}) copy-start(f32[2,24]{1,0:T(2,128)} %param.50) | copy-start | bytes 580
  544.7 15.9 %copy-start.42 = (f32[768]{0:T(1024)S(1)}, f32[768]{0:T(1024)}, u32[]{:S(2)}) copy-start(f32[768]{0:T(1024)} %get-tuple-element.472) | copy-start | bytes 9220
  544.7 37.5 %copy-start.48 = (f32[2,24]{1,0:T(2,128)S(1)}, f32[2,24]{1,0:T(2,128)}, u32[]{:S(2)}) copy-start(f32[2,24]{1,0:T(2,128)} %param.52) | copy-start | bytes 580
  544.7 37.5 %copy-start.49 = (f32[2,24]{1,0:T(2,128)S(1)}, f32[2,24]{1,0:T(2,128)}, u32[]{:S(2)}) copy-start(f32[2,24]{1,0:T(2,128)} %param.51) | copy-start | bytes 580
  547.5 295.6 %all-reduce.15.cloned.1.call-start = ((), (), s32[]{:S(2)}) async-start(), calls=%async_computation.11 | async-start | bytes 6291456 | tf_op jit(solution)/shard_map/psum | solution.py:211
  582.9 7.4 copy-start.38
  583.5 6.9 copy-start.47
  583.5 6.9 copy-start.53
  583.5 6.9 copy-start.54
  583.5 9.0 copy-start.50
  583.5 9.0 copy-start.51
  583.5 12.4 %copy-start.45 = (f32[4,96]{1,0:T(4,128)S(1)}, f32[4,96]{1,0:T(4,128)}, u32[]{:S(2)}) copy-start(f32[4,96]{1,0:T(4,128)} %param.61) | copy-start | bytes 4612
  583.5 12.4 %copy-start.46 = (f32[4,96]{1,0:T(4,128)S(1)}, f32[4,96]{1,0:T(4,128)}, u32[]{:S(2)}) copy-start(f32[4,96]{1,0:T(4,128)} %param.60) | copy-start | bytes 4612
  583.5 36.4 %copy-start.19 = (f32[192,96]{1,0:T(8,128)S(1)}, f32[192,96]{1,0:T(8,128)}, u32[]{:S(2)}) copy-start(f32[192,96]{1,0:T(8,128)} %param.41) | copy-start | bytes 221188
  583.5 36.4 %copy-start.27 = (f32[192,96]{1,0:T(8,128)S(1)}, f32[192,96]{1,0:T(8,128)}, u32[]{:S(2)}) copy-start(f32[192,96]{1,0:T(8,128)} %param.43) | copy-start | bytes 221188
  583.5 36.4 %copy-start.28 = (f32[192,96]{1,0:T(8,128)S(1)}, f32[192,96]{1,0:T(8,128)}, u32[]{:S(2)}) copy-start(f32[192,96]{1,0:T(8,128)} %param.42) | copy-start | bytes 221188
  583.5 107.5 %copy-start.12 = (f32[96,768]{1,0:T(8,128)S(1)}, f32[96,768]{1,0:T(8,128)}, u32[]{:S(2)}) copy-start(f32[96,768]{1,0:T(8,128)} %param.44) | copy-start | bytes 884740
  583.6 107.5 %copy-start.22 = (f32[96,768]{1,0:T(8,128)S(1)}, f32[96,768]{1,0:T(8,128)}, u32[]{:S(2)}) copy-start(f32[96,768]{1,0:T(8,128)} %param.46) | copy-start | bytes 884740
  583.6 107.5 %copy-start.23 = (f32[96,768]{1,0:T(8,128)S(1)}, f32[96,768]{1,0:T(8,128)}, u32[]{:S(2)}) copy-start(f32[96,768]{1,0:T(8,128)} %param.45) | copy-start | bytes 884740
  583.6 179.5 %copy-start.11 = (f32[768,96]{0,1:T(8,128)S(1)}, f32[768,96]{0,1:T(8,128)}, u32[]{:S(2)}) copy-start(f32[768,96]{0,1:T(8,128)} %param.47) | copy-start | bytes 884740
  583.6 179.5 %copy-start.24 = (f32[768,96]{0,1:T(8,128)S(1)}, f32[768,96]{0,1:T(8,128)}, u32[]{:S(2)}) copy-start(f32[768,96]{0,1:T(8,128)} %param.49) | copy-start | bytes 884740
  593.1 1.9 copy-start.40
  621.2 278.9 %copy-start.20 = (f32[192,96]{1,0:T(8,128)}, f32[192,96]{1,0:T(8,128)S(1)}, u32[]{:S(2)}) copy-start(f32[192,96]{1,0:T(8,128)S(1)} %get-tuple-element.444) | copy-start | bytes 221188
  692.8 206.5 %copy-start.14 = (f32[96,768]{1,0:T(8,128)}, f32[96,768]{1,0:T(8,128)S(1)}, u32[]{:S(2)}) copy-start(f32[96,768]{1,0:T(8,128)S(1)} %get-tuple-element.442) | copy-start | bytes 884740
  692.8 206.5 %copy-start.15 = (f32[96,768]{1,0:T(8,128)}, f32[96,768]{1,0:T(8,128)S(1)}, u32[]{:S(2)}) copy-start(f32[96,768]{1,0:T(8,128)S(1)} %get-tuple-element.443) | copy-start | bytes 884740
  843.1 47.6 %copy-start.41 = (f32[2,96]{1,0:T(2,128)S(1)}, f32[2,96]{1,0:T(2,128)}, u32[]{:S(2)}) copy-start(f32[2,96]{1,0:T(2,128)} %copy-done.40) | copy-start | bytes 2308
  843.1 48.2 %copy-start.39 = (f32[2,24]{1,0:T(2,128)S(1)}, f32[2,24]{1,0:T(2,128)}, u32[]{:S(2)}) copy-start(f32[2,24]{1,0:T(2,128)} %copy-done.38) | copy-start | bytes 580
  843.1 55.3 %copy-start.16 = (f32[768,96]{0,1:T(8,128)S(1)}, f32[768,96]{0,1:T(8,128)}, u32[]{:S(2)}) copy-start(f32[768,96]{0,1:T(8,128)} %get-tuple-element.440) | copy-start | bytes 884740
  843.1 55.3 %copy-start.17 = (f32[768,96]{0,1:T(8,128)S(1)}, f32[768,96]{0,1:T(8,128)}, u32[]{:S(2)}) copy-start(f32[768,96]{0,1:T(8,128)} %get-tuple-element.441) | copy-start | bytes 884740
  843.1 57.0 %copy-start.21 = (f32[192,96]{1,0:T(8,128)S(1)}, f32[192,96]{1,0:T(8,128)}, u32[]{:S(2)}) copy-start(f32[192,96]{1,0:T(8,128)} %get-tuple-element.445) | copy-start | bytes 221188
  (9 other events, 11.1 us)
Sparse Core Ops, SparseCore 0:
  143.6 65.7 all-reduce.8
  242.1 68.5 all-reduce.10
  340.1 68.5 all-reduce.12
  590.4 65.0 all-reduce.14
Sparse Core Ops, SparseCore 1:
  146.7 38.5 all-gather.5
  187.9 40.1 all-gather.7
  428.2 61.6 reduce-scatter.23
  493.2 60.6 reduce-scatter.25
  557.2 61.6 reduce-scatter.21
  622.8 68.2 reduce-scatter.15
  694.8 68.2 reduce-scatter.17
  766.8 65.8 reduce-scatter.19
where the time goes:
time: 916 us; the launch traced here: 908 us
  waiting for transfers between devices  356 us (39%)
  blocking collectives  202 us (22%)
  matrix products  136 us (15%)
  local copies, waits for them, and re-layouts  98.7 us (11%)
  other arithmetic  85.6 us (9%)
  between operations  28.7 us (3%)
    unnamed x16, waiting for transfers between devices  80 us
    reduce_scatter x1, waiting for transfers between devices, on_device(): lax.psum_scatter(down_grad, 'dp', scatter_dimension=1, tiled=True)  70.3 us
    reduce_scatter x1, waiting for transfers between devices, on_device(): lax.psum_scatter(up_grad, 'dp', scatter_dimension=0, tiled=True)  69.8 us
    psum x1, waiting for transfers between devices, on_device(): lax.psum(ffn_part.astype(jnp.bfloat16), 'tensor').astype(jnp.float32)  68.4 us
    psum x1, waiting for transfers between devices, on_device(): lax.psum(normed_part.astype(jnp.bfloat16), 'tensor').astype(jnp.float32)  66.1 us
    psum x1, blocking collectives, on_device(): lax.psum(jnp.stack([jnp.stack(weight_sq), jnp.stack(update_sq)]), ('dp',...  39.4 us
    unnamed x2, blocking collectives  39.3 us
    all_gather x1, blocking collectives, on_device(): lax.all_gather(attn_weight.astype(bfloat), 'dp', axis=1, tiled=True)  38.6 us
  transfers between devices with their start and end apart: 12, of which 7 were waited for; matrix products, arithmetic and copies ran while one was open for 22% of the time, Pallas kernels for 0%

commit v1 on v0

--- a/solution.py
+++ b/solution.py
@@ -269,7 +269,7 @@
         weight_sq.extend(square_sums(master, piece_count, weight_factor))
         update_sq.extend(square_sums(update, piece_count, weight_factor))
     square_totals = lax.psum(
-        jnp.stack([jnp.stack(weight_sq), jnp.stack(update_sq)]), ("dp", "tensor")
+        lax.psum(jnp.stack([jnp.stack(weight_sq), jnp.stack(update_sq)]), "tensor"), "dp"
     )
     norm_pairs = jnp.sqrt(square_totals)
     trust = norm_pairs[0] / (norm_pairs[1] + 1e-06)

time: 916 us -> 903 us (0.986)
  blocking collectives: 202 us -> 187 us
  waiting for transfers between devices: 356 us -> 345 us
    psum x1 -> x2, blocking collectives: 39.4 us -> 24.9 us  [the longest x1 19.2 us: on_device(): lax.psum(lax.psum(jnp.stack([jnp.stack(weight_sq), jnp.stack(update_sq)])...]
    unnamed x145 -> x123, local copies, waits for them, and re-layouts: 33.3 us -> 33.3 us
  transfers between devices with their start and end apart: 12 -> 12, of which waited for: 7 -> 7; matrix products, arithmetic and copies ran while one was open for 22% -> 23% of each run, Pallas kernels for 0% -> 0%
where the time goes in v1:
time: 903 us; the launch traced here: 895 us
  waiting for transfers between devices  345 us (38%)
  blocking collectives  187 us (21%)
  matrix products  141 us (16%)
  local copies, waits for them, and re-layouts  99.1 us (11%)
  other arithmetic  92.3 us (10%)
  between operations  28.6 us (3%)
    unnamed x16, waiting for transfers between devices  77.4 us
    reduce_scatter x1, waiting for transfers between devices, on_device(): lax.psum_scatter(down_grad, 'dp', scatter_dimension=1, tiled=True)  70.1 us
    psum x1, waiting for transfers between devices, on_device(): lax.psum(ffn_part.astype(jnp.bfloat16), 'tensor').astype(jnp.float32)  68.2 us
    psum x1, waiting for transfers between devices, on_device(): lax.psum(normed_part.astype(jnp.bfloat16), 'tensor').astype(jnp.float32)  66.1 us
    reduce_scatter x1, waiting for transfers between devices, on_device(): lax.psum_scatter(up_grad, 'dp', scatter_dimension=0, tiled=True)  62.4 us
    unnamed x2, blocking collectives  39.4 us
    all_gather x1, blocking collectives, on_device(): lax.all_gather(attn_weight.astype(bfloat), 'dp', axis=1, tiled=True)  38.6 us
    unnamed x123, local copies, waits for them, and re-layouts  33.3 us
  transfers between devices with their start and end apart: 12, of which 7 were waited for; matrix products, arithmetic and copies ran while one was open for 23% of the time, Pallas kernels for 0%

profile of v1, /device:TPU:0, one launch (start us, length us, event | category | flops | bytes accessed | tf_op | source)
XLA Modules:
  0.0 895.4 jit_solution(11961597100300347600)
XLA Ops:
  9.2 38.6 %all_gather.24 = bf16[3,768,192]{2,0,1:T(4,128)(2,1)S(1)} all-gather(bf16[3,96,192]{2,0,1:T(4,128)(2,1)S(1)} %copy.160), channel_id=1, replica_groups=mesh['dp'=8,'tensor'=4] {'dp'}, dimensions={1}, use_global_device_ids=true | all-gather | bytes 995328 | tf_op jit(solution)/shard_map/all_gather | solution.py:129
  49.0 4.6 convolution_bitcast_fusion
  54.9 2.2 squeeze.31
  57.1 2.2 squeeze.32
  59.4 18.9 %all-gather = bf16[8,24,2]{1,2,0:T(2,128)(2,1)S(1)} all-gather(bf16[1,24,2]{1,2,0:T(2,128)(2,1)S(1)} %convert_bitcast_fusion.2), channel_id=1, replica_groups=mesh['dp'=8,'tensor'=4] {'dp'}, dimensions={0}, use_global_device_ids=true | all-gather | bytes 864 | tf_op jit(solution)/shard_map/all_gather | solution.py:133
  78.5 2.3 convert_element_type.154
  82.1 3.8 fusion.72
  86.9 19.2 %while.26 = (s32[]{:T(128)}, bf16[4,512,3,64]{1,3,2,0:T(8,128)(2,1)}, f32[4,3,512,1]{2,1,3,0:T(4,128)}, bf16[4,512,3,64]{1,3,2,0:T(8,128)(2,1)}, pred[4,512,512]...) while((s32[]{:T(128)}, ...), condition=%wide.region_4.5_spmd, body=%wide.region_1.4_spmd.sunk | while | flops 210860544 | bytes 11588185 | solution.py:149
  89.0 2.7 fusion.159
  93.8 2.7 fusion.159
  98.6 2.7 fusion.159
  103.5 2.7 fusion.159
  112.6 31.2 %all_gather.26 = bf16[192,768]{0,1:T(8,128)(2,1)S(1)} all-gather(bf16[192,96]{0,1:T(8,128)(2,1)} %copy.167), channel_id=1, replica_groups=mesh['dp'=8,'tensor'=4] {'dp'}, dimensions={1}, use_global_device_ids=true | all-gather | bytes 331776 | tf_op jit(solution)/shard_map/all_gather | solution.py:130
  143.8 3.9 convolution_convert_fusion.2
  151.3 16.5 %all-gather.1 = bf16[8,96,4]{1,2,0:T(4,128)(2,1)S(1)} all-gather(bf16[1,96,4]{1,2,0:T(4,128)(2,1)S(1)} %convert_bitcast_fusion), channel_id=1, replica_groups=mesh['dp'=8,'tensor'=4] {'dp'}, dimensions={0}, use_global_device_ids=true | all-gather | bytes 6912 | tf_op jit(solution)/shard_map/all_gather | solution.py:136
  170.6 18.0 %all-gather.2 = bf16[8,96,2]{1,2,0:T(2,128)(2,1)S(1)} all-gather(bf16[1,96,2]{1,2,0:T(2,128)(2,1)S(1)} %convert_bitcast_fusion.1), channel_id=1, replica_groups=mesh['dp'=8,'tensor'=4] {'dp'}, dimensions={0}, use_global_device_ids=true | all-gather | bytes 3456 | tf_op jit(solution)/shard_map/all_gather | solution.py:135
  194.2 17.7 %all-reduce = bf16[768]{0:T(1024)(128)(2,1)S(1)} all-reduce(bf16[768]{0:T(1024)(128)(2,1)S(1)} %dynamic-update-slice), channel_id=1, replica_groups=mesh['dp'=8,'tensor'=4] {'dp'}, use_global_device_ids=true, to_apply=%add | all-reduce | flops 768 | bytes 3072
  213.6 3.1 fusion.68
  219.1 20.6 %multiply_convert_fusion.1 = (bf16[2048,768]{1,0:T(8,128)(2,1)}, f32[2048,768]{1,0:T(8,128)}, f32[2048,768]{1,0:T(8,128)}) fusion(f32[768]{0:T(1024)} %convert_element_type.165, bf16[768,768]{1,0:T(8,128)(2,1)} %all-gather.6.cloned.1.call-done, f32[768]{0:T(1024)} %get-tuple-element.367, f32[768]{0:T(1024)S(1)} %get-tuple-element.370, ...), kind=kOutput, calls=%fused_computation.83 | convolution fusion | flops 2533883904 | bytes 23228416 | tf_op jit(solution)/shard_map/dot_general | solution.py:158
  239.7 6.5 convolution_convert_fusion.1
  246.7 68.2 %all-reduce.11.cloned.1.call-done = bf16[2048,768]{1,0:T(8,128)(2,1)} async-done(((bf16[2048,768]{1,0:T(8,128)(2,1)}), bf16[2048,768]{1,0:T(8,128)(2,1)}) %all-reduce.11.cloned.1.call-update) | async-done | bytes 3145744 | tf_op jit(solution)/shard_map/psum | solution.py:164
  314.9 4.8 fusion.119
  321.7 3.6 fusion.61
  325.3 3.8 fusion.58
  329.1 9.4 %convert_reduce_fusion.1 = (f32[768]{0:T(1024)}, bf16[2048,768]{1,0:T(8,128)(2,1)S(1)}) fusion(f32[2048,768]{1,0:T(8,128)S(1)} %bitcast.250, bf16[768,768]{0,1:T(8,128)(2,1)S(1)} %copy-done.46, f32[2048,768]{1,0:T(8,128)S(1)} %get-tuple-element.457, f32[2048,768]{1,0:T(8,128)} %get-tuple-element.471, f32[768]{0:T(1024)S(1)} %copy-done.41), kind=kOutput, calls=%fused_computation.74 | convolution fusion | flops 2444229888 | bytes 23205888 | tf_op jit(solution)/shard_map/td,fd->tf/dot_general | solution.py:176
  340.2 4.0 convolution_convert_fusion
  346.8 66.1 %all-reduce.13.cloned.1.call-done = bf16[2048,768]{1,0:T(8,128)(2,1)} async-done(((bf16[2048,768]{1,0:T(8,128)(2,1)}), bf16[2048,768]{1,0:T(8,128)(2,1)}) %all-reduce.13.cloned.1.call-update) | async-done | bytes 3145744 | tf_op jit(solution)/shard_map/psum | solution.py:181
  412.9 7.3 multiply_reduce_fusion.1
  420.3 8.1 fusion.111
  432.6 4.9 convolution_convert_fusion.3
  437.5 3.0 reshape.246
  445.5 51.1 %while.27 = (s32[]{:T(128)}, bf16[4,512,3,64]{1,3,2,0:T(8,128)(2,1)}, bf16[4,512,3,64]{1,3,2,0:T(8,128)(2,1)}, bf16[4,512,3,64]{1,3,2,0:T(8,128)(2,1)}, bf16[4,5...) while((s32[]{:T(128)}, ...), condition=%wide.region_18.19_spmd, body=%wide.region_16.18_spmd.sunk | while | flops 510884352 | bytes 26381428 | solution.py:193
  451.9 2.2 fusion.170
  456.1 2.2 fusion.171
  464.7 2.2 fusion.170
  468.9 2.2 fusion.171
  481.6 2.2 fusion.171
  490.2 2.2 fusion.170
  494.4 2.2 fusion.171
  497.7 5.3 fusion.86
  503.0 2.6 copy.172
  505.6 2.8 stack_reshape.9
  510.8 2.7 copy.173
  513.5 2.8 stack_reshape.10
  516.3 2.7 copy.174
  518.9 2.8 stack_reshape.11
  526.0 6.5 bitcast_convert_fusion
  532.6 7.7 fusion.91
  540.7 7.9 fusion.77
  552.7 4.9 fusion.83
  557.6 3.0 copy.187
  560.6 2.8 reshape.264
  573.1 21.7 %all-reduce.3 = (f32[2,192]{1,0:T(2,128)S(1)}, f32[768]{0:T(1024)S(1)}) all-reduce(f32[2,192]{1,0:T(2,128)S(1)} %pad_maximum_fusion.2, f32[768]{0:T(1024)} %get-tuple-element.472), channel_id=6, replica_groups=mesh['dp'=8,'tensor'=4] {'dp'}, use_global_device_ids=true, to_apply=%region_47.48.clone | all-reduce | flops 1152 | bytes 9216
  608.1 16.3 %reduce-scatter.22.cloned.1.call-done = f32[96,192]{1,0:T(8,128)} async-done(((f32[768,192]{1,0:T(8,128)}), f32[96,192]{1,0:T(8,128)}) %reduce-scatter.22.cloned.1.call-update) | async-done | bytes 73744
  625.5 2.3 multiply_reduce_fusion.11
  627.8 6.2 add_convert_fusion
  634.0 62.4 %reduce-scatter.16.cloned.1.call-done = f32[96,768]{1,0:T(8,128)} async-done(((f32[768,768]{1,0:T(8,128)}), f32[96,768]{1,0:T(8,128)}) %reduce-scatter.16.cloned.1.call-update) | async-done | bytes 294928 | tf_op jit(solution)/shard_map/reduce_scatter | solution.py:218
  698.2 70.1 %reduce-scatter.18.cloned.1.call-done = f32[768,96]{0,1:T(8,128)} async-done(((f32[768,768]{0,1:T(8,128)}), f32[768,96]{0,1:T(8,128)}) %reduce-scatter.18.cloned.1.call-update) | async-done | bytes 294928 | tf_op jit(solution)/shard_map/reduce_scatter | solution.py:219
  768.3 2.6 multiply_reduce_fusion.8
  770.8 6.2 stack.157
  777.1 60.9 %reduce-scatter.20.cloned.1.call-done = f32[96,576]{1,0:T(8,128)} async-done(((f32[768,576]{1,0:T(8,128)}), f32[96,576]{1,0:T(8,128)}) %reduce-scatter.20.cloned.1.call-update) | async-done | bytes 221200
  841.8 5.8 stack.185
  848.2 5.6 psum.46
  853.8 19.2 %psum.47 = f32[2,15]{1,0:T(2,128)S(1)} all-reduce(f32[2,15]{1,0:T(2,128)S(1)} %psum.46), channel_id=1, replica_groups=mesh['dp'=8,'tensor'=4] {'dp'}, use_global_device_ids=true, to_apply=%region_68.69 | all-reduce | flops 30 | bytes 240 | tf_op jit(solution)/shard_map/psum | solution.py:271
  (278 shorter events, 133.4 us)
Async XLA Ops:
  8.0 205.6 %all-reduce.9.cloned.1.call-start = ((), (), s32[]{:S(2)}) async-start(), calls=%async_computation.6 | async-start | bytes 6291456 | tf_op jit(solution)/shard_map/psum | solution.py:153
  47.8 1.2 copy-start.13
  53.7 5.7 copy-start.37
  53.9 27.1 %copy-start.25 = (s32[4,512]{1,0:T(4,128)S(1)}, s32[4,512]{1,0:T(4,128)}, u32[]{:S(2)}) copy-start(s32[4,512]{1,0:T(4,128)} %param.37) | copy-start | bytes 24580
  53.9 27.1 %copy-start.42 = (s32[4,64]{1,0:T(4,128)S(1)}, s32[4,64]{1,0:T(4,128)}, u32[]{:S(2)}) copy-start(s32[4,64]{1,0:T(4,128)} %param.36) | copy-start | bytes 3076
  53.9 27.2 %copy-start.44 = (s32[4]{0:T(128)S(1)}, s32[4]{0:T(128)}, u32[]{:S(2)}) copy-start(s32[4]{0:T(128)} %param.35) | copy-start | bytes 52
  86.9 25.0 %copy-start.16 = (f32[192,96]{1,0:T(8,128)S(1)}, f32[192,96]{1,0:T(8,128)}, u32[]{:S(2)}) copy-start(f32[192,96]{1,0:T(8,128)} %param.41) | copy-start | bytes 221188
  106.1 0.9 copy-start.4
  107.0 0.9 copy-start.5
  107.9 1.0 copy-start.6
  109.0 42.3 %copy-start.27 = (f32[4,96]{1,0:T(4,128)S(1)}, f32[4,96]{1,0:T(4,128)}, u32[]{:S(2)}) copy-start(f32[4,96]{1,0:T(4,128)} %param.59) | copy-start | bytes 4612
  109.0 104.6 %copy-start = (bf16[2048,768]{1,0:T(8,128)(2,1)S(1)}, bf16[2048,768]{1,0:T(8,128)(2,1)}, u32[]{:S(2)}) copy-start(bf16[2048,768]{1,0:T(8,128)(2,1)} %param.33) | copy-start | bytes 9437188
  147.7 71.4 %all-gather.6.cloned.1.call-start = ((), (), s32[]{:S(2)}) async-start(), calls=%async_computation.7 | async-start | bytes 1327104 | tf_op jit(solution)/shard_map/all_gather | solution.py:131
  149.4 90.3 %all-gather.8.cloned.1.call-start = ((), (), s32[]{:S(2)}) async-start(), calls=%async_computation.8 | async-start | bytes 1327104 | tf_op jit(solution)/shard_map/all_gather | solution.py:132
  151.2 163.8 %all-reduce.11.cloned.1.call-start = ((), (), s32[]{:S(2)}) async-start(), calls=%async_computation.9 | async-start | bytes 6291456 | tf_op jit(solution)/shard_map/psum | solution.py:164
  213.6 3.2 copy-start.1
  246.2 166.7 %all-reduce.13.cloned.1.call-start = ((), (), s32[]{:S(2)}) async-start(), calls=%async_computation.10 | async-start | bytes 6291456 | tf_op jit(solution)/shard_map/psum | solution.py:181
  319.8 1.9 copy-start.7
  319.8 1.9 copy-start.26
  320.7 4.6 copy-start.30
  321.7 7.5 slice-start
  325.3 3.8 copy-start.41
  325.3 3.8 copy-start.46
  325.3 3.8 slice-start.1
  329.1 9.4 %copy-start.3 = (f32[2048,768]{1,0:T(8,128)}, f32[2048,768]{1,0:T(8,128)S(1)}, u32[]{:S(2)}) copy-start(f32[2048,768]{1,0:T(8,128)S(1)} %get-tuple-element.457) | copy-start | bytes 18874372
  329.1 11.1 %copy-start.45 = (bf16[768,768]{1,0:T(8,128)(2,1)S(1)}, bf16[768,768]{1,0:T(8,128)(2,1)}, u32[]{:S(2)}) copy-start(bf16[768,768]{1,0:T(8,128)(2,1)} %all-gather.6.cloned.1.call-done) | copy-start | bytes 3538948
  338.5 1.7 copy-start.47
  344.2 254.4 %reduce-scatter.24.cloned.1.call-start = ((), (), s32[]{:S(2)}) async-start(), calls=%async_computation.16 | async-start | bytes 442368
  412.9 7.3 copy-start.2
  412.9 7.3 copy-start.8
  412.9 7.3 copy-start.23
  420.2 9.9 %copy-start.35 = (f32[1,768]{1,0:T(1,128)S(1)}, f32[1,768]{1,0:T(1,128)}, u32[]{:S(2)}) copy-start(f32[1,768]{1,0:T(1,128)} %stack.172) | copy-start | bytes 9220
  432.4 170.4 %reduce-scatter.26.cloned.1.call-start = ((), (), s32[]{:S(2)}) async-start(), calls=%async_computation.17 | async-start | bytes 442368
  445.5 51.1 %copy-start.31 = (f32[1,768]{1,0:T(1,128)S(1)}, f32[1,768]{1,0:T(1,128)}, u32[]{:S(2)}) copy-start(f32[1,768]{1,0:T(1,128)} %stack.179) | copy-start | bytes 9220
  445.5 51.1 %copy-start.32 = (f32[1,768]{1,0:T(1,128)S(1)}, f32[1,768]{1,0:T(1,128)}, u32[]{:S(2)}) copy-start(f32[1,768]{1,0:T(1,128)} %stack.176) | copy-start | bytes 9220
  445.5 51.1 %copy-start.33 = (f32[1,768]{1,0:T(1,128)S(1)}, f32[1,768]{1,0:T(1,128)}, u32[]{:S(2)}) copy-start(f32[1,768]{1,0:T(1,128)} %stack.177) | copy-start | bytes 9220
  445.5 51.1 %copy-start.34 = (f32[1,768]{1,0:T(1,128)S(1)}, f32[1,768]{1,0:T(1,128)}, u32[]{:S(2)}) copy-start(f32[1,768]{1,0:T(1,128)} %stack.178) | copy-start | bytes 9220
  497.6 126.8 %reduce-scatter.22.cloned.1.call-start = ((), (), s32[]{:S(2)}) async-start(), calls=%async_computation.15 | async-start | bytes 884736
  508.5 119.3 %all-reduce.15.cloned.1.call-start = ((), (), s32[]{:S(2)}) async-start(), calls=%async_computation.11 | async-start | bytes 6291456 | tf_op jit(solution)/shard_map/psum | solution.py:211
  526.0 6.6 copy-start.24
  526.0 6.6 copy-start.29
  532.5 163.8 %reduce-scatter.16.cloned.1.call-start = ((), (), s32[]{:S(2)}) async-start(), calls=%async_computation.12 | async-start | bytes 2654208 | tf_op jit(solution)/shard_map/reduce_scatter | solution.py:218
  540.4 8.3 copy-start.9
  540.4 9.2 %copy-start.28 = (f32[4,96]{1,0:T(4,128)S(1)}, f32[4,96]{1,0:T(4,128)}, u32[]{:S(2)}) copy-start(f32[4,96]{1,0:T(4,128)} %param.59) | copy-start | bytes 4612
  540.4 227.9 %reduce-scatter.18.cloned.1.call-start = ((), (), s32[]{:S(2)}) async-start(), calls=%async_computation.13 | async-start | bytes 2654208 | tf_op jit(solution)/shard_map/reduce_scatter | solution.py:219
  548.6 289.4 %reduce-scatter.20.cloned.1.call-start = ((), (), s32[]{:S(2)}) async-start(), calls=%async_computation.14 | async-start | bytes 2211840
  557.6 5.8 copy-start.36
  557.6 11.3 %copy-start.38 = (f32[2,24]{1,0:T(2,128)S(1)}, f32[2,24]{1,0:T(2,128)}, u32[]{:S(2)}) copy-start(f32[2,24]{1,0:T(2,128)} %param.50) | copy-start | bytes 580
  560.6 64.8 %copy-start.17 = (f32[192,96]{1,0:T(8,128)S(1)}, f32[192,96]{1,0:T(8,128)}, u32[]{:S(2)}) copy-start(f32[192,96]{1,0:T(8,128)} %param.41) | copy-start | bytes 221188
  596.1 6.6 copy-start.39
  600.8 24.6 %copy-start.40 = (f32[2,96]{1,0:T(2,128)}, f32[2,96]{1,0:T(2,128)S(1)}, u32[]{:S(2)}) copy-start(f32[2,96]{1,0:T(2,128)S(1)} %get-tuple-element.430) | copy-start | bytes 2308
  627.7 258.7 %copy-start.18 = (f32[192,96]{1,0:T(8,128)}, f32[192,96]{1,0:T(8,128)S(1)}, u32[]{:S(2)}) copy-start(f32[192,96]{1,0:T(8,128)S(1)} %get-tuple-element.444) | copy-start | bytes 221188
  627.7 68.6 %copy-start.12 = (f32[96,768]{1,0:T(8,128)S(1)}, f32[96,768]{1,0:T(8,128)}, u32[]{:S(2)}) copy-start(f32[96,768]{1,0:T(8,128)} %param.44) | copy-start | bytes 884740
  627.7 68.6 %copy-start.19 = (f32[96,768]{1,0:T(8,128)S(1)}, f32[96,768]{1,0:T(8,128)}, u32[]{:S(2)}) copy-start(f32[96,768]{1,0:T(8,128)} %param.46) | copy-start | bytes 884740
  627.7 68.7 %copy-start.20 = (f32[96,768]{1,0:T(8,128)S(1)}, f32[96,768]{1,0:T(8,128)}, u32[]{:S(2)}) copy-start(f32[96,768]{1,0:T(8,128)} %param.45) | copy-start | bytes 884740
  627.7 140.5 %copy-start.11 = (f32[768,96]{0,1:T(8,128)S(1)}, f32[768,96]{0,1:T(8,128)}, u32[]{:S(2)}) copy-start(f32[768,96]{0,1:T(8,128)} %param.47) | copy-start | bytes 884740
  627.7 140.5 %copy-start.21 = (f32[768,96]{0,1:T(8,128)S(1)}, f32[768,96]{0,1:T(8,128)}, u32[]{:S(2)}) copy-start(f32[768,96]{0,1:T(8,128)} %param.49) | copy-start | bytes 884740
  627.7 140.5 %copy-start.22 = (f32[768,96]{0,1:T(8,128)S(1)}, f32[768,96]{0,1:T(8,128)}, u32[]{:S(2)}) copy-start(f32[768,96]{0,1:T(8,128)} %param.48) | copy-start | bytes 884740
  627.7 212.2 %copy-start.10 = (f32[3,96,192]{1,2,0:T(8,128)S(1)}, f32[3,96,192]{1,2,0:T(8,128)}, u32[]{:S(2)}) copy-start(f32[3,96,192]{1,2,0:T(8,128)} %copy.179) | copy-start | bytes 663556
  698.2 189.8 %copy-start.14 = (f32[96,768]{1,0:T(8,128)}, f32[96,768]{1,0:T(8,128)S(1)}, u32[]{:S(2)}) copy-start(f32[96,768]{1,0:T(8,128)S(1)} %get-tuple-element.442) | copy-start | bytes 884740
  698.2 189.8 %copy-start.15 = (f32[96,768]{1,0:T(8,128)}, f32[96,768]{1,0:T(8,128)S(1)}, u32[]{:S(2)}) copy-start(f32[96,768]{1,0:T(8,128)S(1)} %get-tuple-element.443) | copy-start | bytes 884740
  873.1 14.9 %copy-start.43 = (f32[2,15]{1,0:T(2,128)}, f32[2,15]{1,0:T(2,128)S(1)}, u32[]{:S(2)}) copy-start(f32[2,15]{1,0:T(2,128)S(1)} %sqrt.35) | copy-start | bytes 364
Sparse Core Ops, SparseCore 0:
  147.8 65.7 all-reduce.8
  246.4 68.5 all-reduce.10
  344.3 68.5 all-reduce.12
  532.6 68.5 all-reduce.14
Sparse Core Ops, SparseCore 1:
  150.9 38.5 all-gather.5
  192.1 40.2 all-gather.7
  432.4 61.7 reduce-scatter.23
  497.7 61.5 reduce-scatter.25
  562.6 61.8 reduce-scatter.21
  628.4 67.9 reduce-scatter.15
  700.1 68.1 reduce-scatter.17
  772.0 65.9 reduce-scatter.19
